TPU v7x, 512 devices: a whole 4x4x16 slice. The times are simulated.
512 devices in a mesh: grp: 64 (over x, z), dev: 8 (over y, core).
Axes of the slice: x: 4, y: 4, z: 16, core: 2. Of those that a mesh axis runs over, the one named last changes fastest.
Arguments:
- tokens: bfloat16 [32768, 768], P(('grp', 'dev')), may hold values from -6 to 6
- expert_ids: int32 [32768, 8], P(('grp', 'dev')), may hold values from 0 to 511, as said below
- gates: bfloat16 [32768, 8], P(('grp', 'dev')), may hold values from 0.099609375 to 0.5
- w_in: bfloat16 [512, 768, 1536], P(('grp', 'dev')), may hold values from -0.21875 to 0.21875
- w_out: bfloat16 [512, 1536, 768], P(('grp', 'dev')), may hold values from -0.15625 to 0.15625
Outputs:
- mixed: bfloat16 [32768, 768], P(('grp', 'dev'))
Inputs may be any that keep to these rules, and one draw needn't show every extreme that they name: `expert_ids`: row t lists 8 experts; columns 2 * k and 2 * k + 1 are two different experts of one group (experts g * 8 to g * 8 + 7 form group g), and the four groups of a row differ. The owner of token t is t // 64, and its dev index is the owner modulo 8. The tokens of one owner pick one group at most 12 times, and every owner reaches it for some group. The tokens whose owners share a dev index pick each group exactly 4 * 64 times in all and each expert at most 192 times; in every group one expert is picked 192 times by the tokens of every dev index.
All inputs are finite; a program needn't handle non-finite values.
Results may differ from a plain program's by a relative error of at most 0.0057.
Values may be sent and summed in bfloat16 or wider, within the bound.
A program may use at most 64 MiB of HBM per device.

v0:
```python
import jax
import jax.numpy as jnp
from jax import lax
from jax.sharding import PartitionSpec as P

F32 = jnp.float32
BF16 = jnp.bfloat16
NX = 4
NZ = 16


def per_device(tokens, expert_ids, gates, w_in, w_out):
    n_dev = lax.axis_size("dev")
    count, width = tokens.shape
    cap = 4 * count
    z_sets = [[x * NZ + z for z in range(NZ)] for x in range(NX)]
    x_sets = [[x * NZ + z for x in range(NX)] for z in range(NZ)]
    me = lax.axis_index("grp")
    my_x, my_z = (me // NZ, me % NZ)
    mine = lax.axis_index("dev")
    pairs = expert_ids.reshape(count, 4, 2)
    gate_pairs = gates.reshape(count, 4, 2)
    meta = jnp.concatenate(
        [
            (pairs[:, :, 0] // n_dev).astype(BF16),
            (pairs[:, :, 0] % n_dev).astype(BF16),
            (pairs[:, :, 1] % n_dev).astype(BF16),
            gate_pairs[:, :, 0],
            gate_pairs[:, :, 1],
        ],
        axis=1,
    ).T
    column = lax.all_gather(tokens, "grp", axis_index_groups=z_sets, tiled=True)
    metas = lax.all_gather(meta, "grp")
    group = metas[:, 0:4, :].astype(jnp.int32)
    tri = (jnp.arange(count)[:, None] < jnp.arange(count)[None, :]).astype(BF16)
    owners = NX * NZ
    tri_o = (jnp.arange(owners)[:, None] < jnp.arange(owners)[None, :]).astype(F32)
    targets = jnp.arange(NX) * NZ + my_z
    match = (group[None] == targets[:, None, None, None]).astype(BF16)
    hit = jnp.sum(match, axis=2)
    within = jnp.dot(hit, tri, preferred_element_type=F32)
    totals = jnp.sum(hit.astype(F32), axis=2)
    base = jnp.dot(totals, tri_o, precision=lax.Precision.HIGHEST)
    place = jnp.where(hit > 0, within + base[:, :, None], -1.0).astype(jnp.int32)
    own = lax.dynamic_slice_in_dim(place, my_x * NZ, NZ, axis=1).reshape(NX, NZ * count)
    rows = jnp.arange(cap)
    select = (own[:, None, :] == rows[None, :, None]).astype(BF16).reshape(NX * cap, NZ * count)
    spread = jnp.dot(select, column, preferred_element_type=F32).astype(BF16)
    group_rows = lax.psum_scatter(
        spread, "grp", scatter_dimension=0, axis_index_groups=x_sets, tiled=True
    )
    all_rows = lax.all_gather(group_rows, "dev", tiled=True)
    place_me = lax.dynamic_index_in_dim(place, my_x, 0, keepdims=False).reshape(-1)
    match_me = lax.dynamic_index_in_dim(match, my_x, 0, keepdims=False)
    facts = jnp.stack(
        [jnp.sum(match_me * metas[:, 4 * i : 4 * i + 4, :], axis=1) for i in range(1, 5)], axis=-1
    ).reshape(owners * count, 4)
    seat = (place_me[None, :] == rows[:, None]).astype(BF16)
    row_facts = jnp.dot(seat, facts, preferred_element_type=F32).astype(BF16)
    all_facts = lax.all_gather(row_facts, "dev", tiled=True)
    who = mine.astype(BF16)
    weight = jnp.where(all_facts[:, 0] == who, all_facts[:, 2], 0).astype(F32) + jnp.where(
        all_facts[:, 1] == who, all_facts[:, 3], 0
    ).astype(F32)
    hidden = jnp.maximum(jnp.dot(all_rows, w_in[0], preferred_element_type=F32), 0.0).astype(BF16)
    out = jnp.dot(hidden, w_out[0], preferred_element_type=F32)
    out = (out * weight[:, None]).astype(BF16)
    group_sum = lax.psum_scatter(out, "dev", scatter_dimension=0, tiled=True)
    back = lax.all_gather(group_sum, "grp", axis_index_groups=x_sets, tiled=True)
    partial_sum = lax.dot_general(
        select, back, (((0,), (0,)), ((), ())), preferred_element_type=F32
    ).astype(BF16)
    return lax.psum_scatter(
        partial_sum, "grp", scatter_dimension=0, axis_index_groups=z_sets, tiled=True
    )


def solution(mesh):
    tok = P(("grp", "dev"), None)
    return jax.shard_map(
        per_device,
        mesh=mesh,
        in_specs=(tok, tok, tok, P(("grp", "dev"), None, None), P(("grp", "dev"), None, None)),
        out_specs=tok,
        check_vma=False,
    )
```

profile of v0, /device:TPU:4, one launch (start us, length us, event | category | flops | bytes accessed | tf_op | source)
XLA Modules:
  0.0 360.3 jit_solution(1277123264415232062)
XLA Ops:
  6.5 0.0 copy-start
  6.5 0.0 all-gather.6.cloned.1.call-start
  6.5 0.7 all-gather.6.cloned.1.call-update
  7.3 0.0 reduce-scatter.4.cloned.1.call-start
  7.4 0.8 fusion.32
  8.1 0.8 fusion.31
  8.9 0.1 concatenate.4
  9.0 99.7 %all-gather.1 = bf16[64,20,64]{2,1,0:T(8,128)(2,1)S(1)} all-gather(bf16[1,20,64]{2,1,0:T(8,128)(2,1)S(1)} %bitcast.41), channel_id=2, replica_groups=mesh['grp'=64,'dev'=8] {'grp'}, dimensions={0}, use_global_device_ids=true | all-gather | bytes 166400 | tf_op jit(solution)/shard_map/all_gather | solution.py:34
  108.8 0.5 fusion.30
  109.2 0.1 convert_reduce_fusion
  109.3 0.1 fusion.18
  109.5 0.2 fusion.5
  109.7 0.1 eq.70
  109.8 1.6 bitcast_compare_fusion
  111.4 0.0 all-gather.6.cloned.1.call-done
  111.4 4.7 %convolution_convert_fusion.1 = bf16[1024,768]{1,0:T(8,128)(2,1)} fusion(pred[1024,1024]{1,0:T(32,128)(4,1)} %bitcast_compare_fusion, bf16[1024,768]{1,0:T(8,128)(2,1)} %all-gather.6.cloned.1.call-done), kind=kOutput, calls=%fused_computation.9 | convolution fusion | flops 1611399168 | bytes 4194304 | tf_op jit(solution)/shard_map/dot_general | solution.py:49
  116.1 0.0 reduce-scatter.4.cloned.1.call-update
  116.1 0.0 all-gather.8.cloned.1.call-start
  116.2 29.0 %reduce-scatter.4.cloned.1.call-done = bf16[256,768]{1,0:T(8,128)(2,1)} async-done(((bf16[1024,768]{1,0:T(8,128)(2,1)}), bf16[256,768]{1,0:T(8,128)(2,1)}) %reduce-scatter.4.cloned.1.call-update) | async-done | bytes 393232 | tf_op jit(solution)/shard_map/reduce_scatter | solution.py:50
  145.1 0.0 all-gather.8.cloned.1.call-update
  145.1 0.0 reduce-scatter.6.cloned.1.call-start
  145.2 0.1 eq.77
  145.3 0.2 compare_convert_fusion
  145.5 0.4 fusion.10
  145.9 0.1 stack.15
  146.0 0.1 stack.17
  146.1 0.1 stack.16
  146.2 0.1 stack.18
  146.3 0.8 fusion.6
  147.1 12.0 %all_gather.22 = bf16[2048,4]{0,1:T(4,128)(2,1)S(1)} all-gather(bf16[256,4]{0,1:T(4,128)(2,1)S(1)} %fusion.6), channel_id=1, replica_groups=mesh['grp'=64,'dev'=8] {'dev'}, dimensions={0}, use_global_device_ids=true | all-gather | bytes 18432 | tf_op jit(solution)/shard_map/all_gather | solution.py:61
  159.1 25.1 %all-gather.8.cloned.1.call-done = bf16[2048,768]{1,0:T(8,128)(2,1)} async-done(((bf16[256,768]{1,0:T(8,128)(2,1)}), bf16[2048,768]{1,0:T(8,128)(2,1)}) %all-gather.8.cloned.1.call-update) | async-done | bytes 3145744 | tf_op jit(solution)/shard_map/all_gather | solution.py:53
  184.1 0.0 copy-done
  184.1 0.0 copy-start.2
  184.1 7.3 %maximum_convert_fusion = bf16[2048,1536]{1,0:T(8,128)(2,1)S(1)} fusion(bf16[2048,768]{1,0:T(8,128)(2,1)} %all-gather.8.cloned.1.call-done, bf16[1,768,1536]{2,1,0:T(8,128)(2,1)S(1)} %copy-done), kind=kOutput, calls=%fused_computation | convolution fusion | flops 4838129664 | bytes 11796480 | tf_op jit(solution)/shard_map/dot_general | solution.py:66
  191.5 0.0 copy-done.2
  191.5 6.4 %multiply_convert_fusion = bf16[2048,768]{1,0:T(8,128)(2,1)} fusion(bf16[2048,1536]{1,0:T(8,128)(2,1)S(1)} %maximum_convert_fusion, f32[2048]{0:T(1024)S(1)} %bitcast.46, bf16[1,1536,768]{2,1,0:T(8,128)(2,1)S(1)} %copy-done.2), kind=kOutput, calls=%fused_computation.1 | convolution fusion | flops 4834983936 | bytes 11804672 | tf_op jit(solution)/shard_map/dot_general | solution.py:67
  197.9 0.0 copy-start.1
  197.9 0.0 reduce-scatter.6.cloned.1.call-update
  197.9 0.0 all-gather.10.cloned.1.call-start
  197.9 43.6 %reduce-scatter.6.cloned.1.call-done = bf16[256,768]{1,0:T(8,128)(2,1)} async-done(((bf16[2048,768]{1,0:T(8,128)(2,1)}), bf16[256,768]{1,0:T(8,128)(2,1)}) %reduce-scatter.6.cloned.1.call-update) | async-done | bytes 393232 | tf_op jit(solution)/shard_map/reduce_scatter | solution.py:69
  241.5 0.0 all-gather.10.cloned.1.call-update
  241.6 0.0 reduce-scatter.8.cloned.1.call-start
  241.6 33.7 %all-gather.10.cloned.1.call-done = bf16[1024,768]{1,0:T(8,128)(2,1)} async-done(((bf16[256,768]{1,0:T(8,128)(2,1)}), bf16[1024,768]{1,0:T(8,128)(2,1)}) %all-gather.10.cloned.1.call-update) | async-done | bytes 1572880 | tf_op jit(solution)/shard_map/all_gather | solution.py:70
  275.3 0.0 copy-done.1
  275.3 4.8 %convolution_convert_fusion = bf16[1024,768]{1,0:T(8,128)(2,1)} fusion(pred[1024,1024]{1,0:T(32,128)(4,1)S(1)} %copy-done.1, bf16[1024,768]{1,0:T(8,128)(2,1)} %all-gather.10.cloned.1.call-done), kind=kOutput, calls=%fused_computation.8 | convolution fusion | flops 1611399168 | bytes 4194304 | tf_op jit(solution)/shard_map/dot_general | solution.py:71
  280.1 0.0 reduce-scatter.8.cloned.1.call-update
  280.2 73.3 %reduce-scatter.8.cloned.1.call-done = bf16[64,768]{1,0:T(8,128)(2,1)} async-done(((bf16[1024,768]{1,0:T(8,128)(2,1)}), bf16[64,768]{1,0:T(8,128)(2,1)}) %reduce-scatter.8.cloned.1.call-update) | async-done | bytes 98320 | tf_op jit(solution)/shard_map/reduce_scatter | solution.py:74
  (9 shorter events, 0.1 us)
Async XLA Ops:
  6.5 177.6 %copy-start = (bf16[1,768,1536]{2,1,0:T(8,128)(2,1)S(1)}, bf16[1,768,1536]{2,1,0:T(8,128)(2,1)}, u32[]{:S(2)}) copy-start(bf16[1,768,1536]{2,1,0:T(8,128)(2,1)} %param.8) | copy-start | bytes 7077892
  6.5 104.9 %all-gather.6.cloned.1.call-start = ((), (), s32[]{:S(2)}) async-start(), calls=%async_computation.3 | async-start | bytes 1671168 | tf_op jit(solution)/shard_map/all_gather | solution.py:33
  7.3 137.9 %reduce-scatter.4.cloned.1.call-start = ((), (), s32[]{:S(2)}) async-start(), calls=%async_computation.4 | async-start | bytes 1966080 | tf_op jit(solution)/shard_map/reduce_scatter | solution.py:50
  116.1 68.0 %all-gather.8.cloned.1.call-start = ((), (), s32[]{:S(2)}) async-start(), calls=%async_computation.5 | async-start | bytes 3538944 | tf_op jit(solution)/shard_map/all_gather | solution.py:53
  145.1 96.4 %reduce-scatter.6.cloned.1.call-start = ((), (), s32[]{:S(2)}) async-start(), calls=%async_computation.6 | async-start | bytes 3538944 | tf_op jit(solution)/shard_map/reduce_scatter | solution.py:69
  184.1 7.3 %copy-start.2 = (bf16[1,1536,768]{2,1,0:T(8,128)(2,1)S(1)}, bf16[1,1536,768]{2,1,0:T(8,128)(2,1)}, u32[]{:S(2)}) copy-start(bf16[1,1536,768]{2,1,0:T(8,128)(2,1)} %param.9) | copy-start | bytes 7077892
  197.9 77.5 %copy-start.1 = (pred[1024,1024]{1,0:T(32,128)(4,1)S(1)}, pred[1024,1024]{1,0:T(32,128)(4,1)}, u32[]{:S(2)}) copy-start(pred[1024,1024]{1,0:T(32,128)(4,1)} %bitcast_compare_fusion) | copy-start | bytes 3145732
  197.9 77.5 %all-gather.10.cloned.1.call-start = ((), (), s32[]{:S(2)}) async-start(), calls=%async_computation.7 | async-start | bytes 1966080 | tf_op jit(solution)/shard_map/all_gather | solution.py:70
  241.6 111.9 %reduce-scatter.8.cloned.1.call-start = ((), (), s32[]{:S(2)}) async-start(), calls=%async_computation.8 | async-start | bytes 1671168 | tf_op jit(solution)/shard_map/reduce_scatter | solution.py:74
Sparse Core Ops, SparseCore 0:
  9.4 76.8 all-gather.5
  116.2 28.8 reduce-scatter.3
  147.2 36.8 all-gather.7
  198.0 43.4 reduce-scatter.5
  243.5 31.8 all-gather.9
  280.3 73.1 reduce-scatter.7
where the time goes:
time: 360 us
  waiting for transfers between devices  205 us (57%)
  blocking collectives  112 us (31%)
  matrix products  24.3 us (7%)
  between operations  13.6 us (4%)
    all_gather x1, blocking collectives, per_device(): metas = lax.all_gather(meta, 'grp')  99.7 us
    reduce_scatter x1, waiting for transfers between devices, per_device(): lax.psum_scatter(partial_sum, 'grp', scatter_dimension=0, axis_index_grou...  73.3 us
    reduce_scatter x1, waiting for transfers between devices, per_device(): group_sum = lax.psum_scatter(out, 'dev', scatter_dimension=0, tiled=True)  43.6 us
    all_gather x1, waiting for transfers between devices, per_device(): lax.all_gather(group_sum, 'grp', axis_index_groups=x_sets, tiled=True)  33.7 us
    reduce_scatter x1, waiting for transfers between devices, per_device(): lax.psum_scatter(spread, 'grp', scatter_dimension=0, axis_index_groups=x_...  29 us
    all_gather x1, waiting for transfers between devices, per_device(): all_rows = lax.all_gather(group_rows, 'dev', tiled=True)  25.1 us
    all_gather x1, blocking collectives, per_device(): all_facts = lax.all_gather(row_facts, 'dev', tiled=True)  12 us
    dot_general x1, matrix products, per_device(): jnp.dot(all_rows, w_in[0], preferred_element_type=F32)  7.32 us
  transfers between devices with their start and end apart: 6, of which 5 were waited for; matrix products, arithmetic and copies ran while one was open for 2% of the time, Pallas kernels for 0%

commit v1 on v0

--- a/solution.py
+++ b/solution.py
@@ -50,7 +50,9 @@
     group_rows = lax.psum_scatter(
         spread, "grp", scatter_dimension=0, axis_index_groups=x_sets, tiled=True
     )
-    all_rows = lax.all_gather(group_rows, "dev", tiled=True)
+    all_rows = jnp.concatenate(
+        lax.all_to_all(jnp.stack([group_rows] * lax.axis_size("dev")), "dev", 0, 0), axis=0
+    )
     place_me = lax.dynamic_index_in_dim(place, my_x, 0, keepdims=False).reshape(-1)
     match_me = lax.dynamic_index_in_dim(match, my_x, 0, keepdims=False)
     facts = jnp.stack(

time: 360 us -> 372 us (1.033)
  the two profiles are of different devices: /device:TPU:4 before, /device:TPU:6 now
where the time goes in v1:
time: 372 us
  waiting for transfers between devices  181 us (49%)
  blocking collectives  140 us (38%)
  matrix products  24.3 us (7%)
  between operations  13.3 us (4%)
  local copies, waits for them, and re-layouts  5.04 us (1%)
  starting transfers between devices  4.6 us (1%)
    all_gather x1, blocking collectives, per_device(): metas = lax.all_gather(meta, 'grp')  99.5 us
    reduce_scatter x1, waiting for transfers between devices, per_device(): lax.psum_scatter(partial_sum, 'grp', scatter_dimension=0, axis_index_grou...  73.3 us
    reduce_scatter x1, waiting for transfers between devices, per_device(): group_sum = lax.psum_scatter(out, 'dev', scatter_dimension=0, tiled=True)  43.4 us
    all_gather x1, blocking collectives, per_device(): all_facts = lax.all_gather(row_facts, 'dev', tiled=True)  41 us
    all_gather x1, waiting for transfers between devices, per_device(): lax.all_gather(group_sum, 'grp', axis_index_groups=x_sets, tiled=True)  33.9 us
    reduce_scatter x1, waiting for transfers between devices, per_device(): lax.psum_scatter(spread, 'grp', scatter_dimension=0, axis_index_groups=x_...  29.9 us
  transfers between devices with their start and end apart: 6, of which 4 were waited for; matrix products, arithmetic and copies ran while one was open for 2% of the time, Pallas kernels for 0%

profile of v1, /device:TPU:6, one launch (start us, length us, event | category | flops | bytes accessed | tf_op | source)
XLA Modules:
  0.0 371.9 jit_solution(7004375505737287326)
XLA Ops:
  6.5 0.0 copy-start
  6.5 0.0 all-gather.5.cloned.1.call-start
  6.5 0.7 all-gather.5.cloned.1.call-update
  7.3 0.0 reduce-scatter.4.cloned.1.call-start
  7.4 0.8 fusion.32
  8.1 0.8 fusion.31
  8.9 0.1 concatenate.4
  9.0 99.5 %all-gather.1 = bf16[64,20,64]{2,1,0:T(8,128)(2,1)S(1)} all-gather(bf16[1,20,64]{2,1,0:T(8,128)(2,1)S(1)} %bitcast.42), channel_id=2, replica_groups=mesh['grp'=64,'dev'=8] {'grp'}, dimensions={0}, use_global_device_ids=true | all-gather | bytes 166400 | tf_op jit(solution)/shard_map/all_gather | solution.py:34
  108.5 0.5 fusion.30
  109.0 0.1 convert_reduce_fusion
  109.1 0.1 fusion.18
  109.2 0.2 fusion.5
  109.4 0.1 eq.70
  109.5 1.7 bitcast_compare_fusion
  111.2 0.0 all-gather.5.cloned.1.call-done
  111.2 4.7 %convolution_convert_fusion.1 = bf16[1024,768]{1,0:T(8,128)(2,1)} fusion(pred[1024,1024]{1,0:T(32,128)(4,1)} %bitcast_compare_fusion, bf16[1024,768]{1,0:T(8,128)(2,1)} %all-gather.5.cloned.1.call-done), kind=kOutput, calls=%fused_computation.9 | convolution fusion | flops 1611399168 | bytes 4194304 | tf_op jit(solution)/shard_map/dot_general | solution.py:49
  115.8 0.0 reduce-scatter.4.cloned.1.call-update
  115.9 29.9 %reduce-scatter.4.cloned.1.call-done = bf16[256,768]{1,0:T(8,128)(2,1)} async-done(((bf16[1024,768]{1,0:T(8,128)(2,1)}), bf16[256,768]{1,0:T(8,128)(2,1)}) %reduce-scatter.4.cloned.1.call-update) | async-done | bytes 393232 | tf_op jit(solution)/shard_map/reduce_scatter | solution.py:50
  145.8 2.9 stack.12
  148.6 4.4 %all-to-all-start = ((bf16[8,256,768]{2,1,0:T(8,128)(2,1)}), bf16[8,256,768]{2,1,0:T(8,128)(2,1)}, u32[]{:S(2)}, u32[]{:S(2)}) async-start(bf16[8,256,768]{2,1,0:T(8,128)(2,1)} %stack.12), calls=%async_computation.1 | async-start | bytes 6291456 | tf_op jit(solution)/shard_map/all_to_all | solution.py:54
  153.1 0.0 reduce-scatter.6.cloned.1.call-start
  153.2 0.1 eq.77
  153.2 0.2 compare_convert_fusion
  153.4 0.4 fusion.10
  153.8 0.1 stack.13
  153.9 0.1 stack.29
  154.0 0.1 stack.28
  154.1 0.1 stack.30
  154.2 0.8 fusion.6
  155.0 41.0 %all_gather.18 = bf16[2048,4]{0,1:T(4,128)(2,1)S(1)} all-gather(bf16[256,4]{0,1:T(4,128)(2,1)S(1)} %fusion.6), channel_id=1, replica_groups=mesh['grp'=64,'dev'=8] {'dev'}, dimensions={0}, use_global_device_ids=true | all-gather | bytes 18432 | tf_op jit(solution)/shard_map/all_gather | solution.py:63
  196.1 0.0 all-to-all-done
  196.1 0.0 copy-done
  196.1 0.0 copy-start.2
  196.1 7.3 %maximum_convert_fusion = bf16[2048,1536]{1,0:T(8,128)(2,1)S(1)} fusion(bf16[2048,768]{1,0:T(8,128)(2,1)} %bitcast.9, bf16[1,768,1536]{2,1,0:T(8,128)(2,1)S(1)} %copy-done), kind=kOutput, calls=%fused_computation | convolution fusion | flops 4838129664 | bytes 11796480 | tf_op jit(solution)/shard_map/dot_general | solution.py:68
  203.5 0.0 copy-done.2
  203.5 6.4 %multiply_convert_fusion = bf16[2048,768]{1,0:T(8,128)(2,1)} fusion(bf16[2048,1536]{1,0:T(8,128)(2,1)S(1)} %maximum_convert_fusion, f32[2048]{0:T(1024)S(1)} %bitcast.47, bf16[1,1536,768]{2,1,0:T(8,128)(2,1)S(1)} %copy-done.2), kind=kOutput, calls=%fused_computation.1 | convolution fusion | flops 4834983936 | bytes 11804672 | tf_op jit(solution)/shard_map/dot_general | solution.py:69
  209.8 0.0 copy-start.1
  209.8 0.0 reduce-scatter.6.cloned.1.call-update
  209.9 0.0 all-gather.7.cloned.1.call-start
  209.9 43.4 %reduce-scatter.6.cloned.1.call-done = bf16[256,768]{1,0:T(8,128)(2,1)} async-done(((bf16[2048,768]{1,0:T(8,128)(2,1)}), bf16[256,768]{1,0:T(8,128)(2,1)}) %reduce-scatter.6.cloned.1.call-update) | async-done | bytes 393232 | tf_op jit(solution)/shard_map/reduce_scatter | solution.py:71
  253.3 0.0 all-gather.7.cloned.1.call-update
  253.3 0.0 reduce-scatter.8.cloned.1.call-start
  253.4 33.9 %all-gather.7.cloned.1.call-done = bf16[1024,768]{1,0:T(8,128)(2,1)} async-done(((bf16[256,768]{1,0:T(8,128)(2,1)}), bf16[1024,768]{1,0:T(8,128)(2,1)}) %all-gather.7.cloned.1.call-update) | async-done | bytes 1572880 | tf_op jit(solution)/shard_map/all_gather | solution.py:72
  287.3 0.0 copy-done.1
  287.3 4.8 %convolution_convert_fusion = bf16[1024,768]{1,0:T(8,128)(2,1)} fusion(pred[1024,1024]{1,0:T(32,128)(4,1)S(1)} %copy-done.1, bf16[1024,768]{1,0:T(8,128)(2,1)} %all-gather.7.cloned.1.call-done), kind=kOutput, calls=%fused_computation.8 | convolution fusion | flops 1611399168 | bytes 4194304 | tf_op jit(solution)/shard_map/dot_general | solution.py:73
  292.1 0.0 reduce-scatter.8.cloned.1.call-update
  292.1 73.3 %reduce-scatter.8.cloned.1.call-done = bf16[64,768]{1,0:T(8,128)(2,1)} async-done(((bf16[1024,768]{1,0:T(8,128)(2,1)}), bf16[64,768]{1,0:T(8,128)(2,1)}) %reduce-scatter.8.cloned.1.call-update) | async-done | bytes 98320 | tf_op jit(solution)/shard_map/reduce_scatter | solution.py:76
  (9 shorter events, 0.1 us)
Async XLA Ops:
  6.5 189.6 %copy-start = (bf16[1,768,1536]{2,1,0:T(8,128)(2,1)S(1)}, bf16[1,768,1536]{2,1,0:T(8,128)(2,1)}, u32[]{:S(2)}) copy-start(bf16[1,768,1536]{2,1,0:T(8,128)(2,1)} %param.8) | copy-start | bytes 7077892
  6.5 104.6 %all-gather.5.cloned.1.call-start = ((), (), s32[]{:S(2)}) async-start(), calls=%async_computation.4 | async-start | bytes 1671168 | tf_op jit(solution)/shard_map/all_gather | solution.py:33
  7.3 138.5 %reduce-scatter.4.cloned.1.call-start = ((), (), s32[]{:S(2)}) async-start(), calls=%async_computation.5 | async-start | bytes 1966080 | tf_op jit(solution)/shard_map/reduce_scatter | solution.py:50
  148.6 47.4 %all-to-all-start = ((bf16[8,256,768]{2,1,0:T(8,128)(2,1)}), bf16[8,256,768]{2,1,0:T(8,128)(2,1)}, u32[]{:S(2)}, u32[]{:S(2)}) async-start(bf16[8,256,768]{2,1,0:T(8,128)(2,1)} %stack.12), calls=%async_computation.1 | async-start | bytes 6291456 | tf_op jit(solution)/shard_map/all_to_all | solution.py:54
  153.1 100.2 %reduce-scatter.6.cloned.1.call-start = ((), (), s32[]{:S(2)}) async-start(), calls=%async_computation.6 | async-start | bytes 3538944 | tf_op jit(solution)/shard_map/reduce_scatter | solution.py:71
  196.1 7.4 %copy-start.2 = (bf16[1,1536,768]{2,1,0:T(8,128)(2,1)S(1)}, bf16[1,1536,768]{2,1,0:T(8,128)(2,1)}, u32[]{:S(2)}) copy-start(bf16[1,1536,768]{2,1,0:T(8,128)(2,1)} %param.9) | copy-start | bytes 7077892
  209.8 77.5 %copy-start.1 = (pred[1024,1024]{1,0:T(32,128)(4,1)S(1)}, pred[1024,1024]{1,0:T(32,128)(4,1)}, u32[]{:S(2)}) copy-start(pred[1024,1024]{1,0:T(32,128)(4,1)} %bitcast_compare_fusion) | copy-start | bytes 3145732
  209.9 77.5 %all-gather.7.cloned.1.call-start = ((), (), s32[]{:S(2)}) async-start(), calls=%async_computation.7 | async-start | bytes 1966080 | tf_op jit(solution)/shard_map/all_gather | solution.py:72
  253.3 112.1 %reduce-scatter.8.cloned.1.call-start = ((), (), s32[]{:S(2)}) async-start(), calls=%async_computation.8 | async-start | bytes 1671168 | tf_op jit(solution)/shard_map/reduce_scatter | solution.py:76
Sparse Core Ops, SparseCore 0:
  9.4 77.0 all-gather.4
  116.0 29.7 reduce-scatter.3
  210.0 43.2 reduce-scatter.5
  255.3 31.9 all-gather.6
  292.3 73.1 reduce-scatter.7
